TPU v7x, 32 devices: a whole 2x2x4 slice. The times are simulated.
32 devices in a mesh: row: 4 (over y, core), col: 8 (over z, x).
Axes of the slice: x: 2, y: 2, z: 4, core: 2. Of those that a mesh axis runs over, the one named last changes fastest.
Arguments:
- points: float32 [4, 4, 256, 128], P(None, 'row'), may hold values from -1 to 1
- rhs: float32 [4, 4, 256, 256], P(None, 'row', None, 'col'), may hold values from -6 to 6
Outputs:
- factored: float32 [4, 4, 256, 2, 8, 256], P(None, 'row', None, None, 'col')
- solved: float32 [4, 4, 256, 256], P(None, 'row', None, 'col')
All inputs are finite; a program needn't handle non-finite values.
Results may differ from a plain program's by a relative error of at most 0.0003.
Values sent between devices are 32-bit elements; how exact they have to be, the bound alone decides.
A program may use at most 64 MiB of HBM per device.

v0:
```python
import jax
import jax.numpy as jnp
from jax import lax
from jax.sharding import PartitionSpec as P

PANELS = 2


SCALE = 3.0
NUGGET = 1.0
HIGHEST = lax.Precision.HIGHEST


def from_root(block, axis, owner):
    block = jnp.where(lax.axis_index(axis) == owner, block, jnp.zeros_like(block))
    return lax.psum(block, axis)


def kernel_tiles(left_points, right_points, left_index, right_index):
    feature_dim = left_points.shape[-1]
    left_sq = jnp.sum(left_points * left_points, axis=-1)
    right_sq = jnp.sum(right_points * right_points, axis=-1)
    inner_prod = jnp.einsum("ipf,jqf->ipjq", left_points, right_points, precision=HIGHEST)
    distance = left_sq[:, :, None, None] + right_sq[None, None, :, :] - 2.0 * inner_prod
    diagonal_hit = (left_index[:, :, None, None] == right_index[None, None, :, :]).astype(
        jnp.float32
    )
    return jnp.exp(-SCALE / feature_dim * distance) + NUGGET * diagonal_hit


def advance(current, panel_tiles, inverse, pivot_rhs, tile_of_row, which_panel):
    answer = jnp.dot(inverse, pivot_rhs, precision=HIGHEST)
    change = jnp.einsum("ipq,qn->ipn", panel_tiles, answer, precision=HIGHEST)
    below_rows = (tile_of_row > which_panel)[:, None, None]
    return (jnp.where(below_rows, current - change, current), answer)


def per_device(points, rhs):
    rows_n = lax.axis_size("row")
    cols_n = lax.axis_size("col")
    row_id = lax.axis_index("row")
    col_id = lax.axis_index("col")
    tile_rows = points.shape[0]
    tile_size = points.shape[2]
    feature_dim = points.shape[3]
    tile_cols = tile_rows * rows_n // cols_n
    stride = cols_n // rows_n
    row_points = points[:, 0]
    tile_of_row = jnp.arange(tile_rows, dtype=jnp.int32) * rows_n + row_id
    tile_of_col = jnp.arange(tile_cols, dtype=jnp.int32) * cols_n + col_id
    offsets = jnp.arange(tile_size, dtype=jnp.int32)
    row_index = tile_of_row[:, None] * tile_size + offsets[None, :]
    col_index = tile_of_col[:, None] * tile_size + offsets[None, :]
    grouped = row_points.reshape(tile_cols, stride, tile_size, feature_dim)
    chosen = lax.dynamic_index_in_dim(grouped, col_id // rows_n, 1, keepdims=False)
    col_points = from_root(chosen, "row", col_id % rows_n)
    kernel_grid = kernel_tiles(row_points, col_points, row_index, col_index)
    current = rhs[:, 0]
    identity = jnp.eye(tile_size, dtype=jnp.float32)
    row_panels = []
    answers = []
    for which_panel in range(PANELS):
        slot_a = which_panel // rows_n
        root_r = which_panel % rows_n
        slot_b = which_panel // cols_n
        root_c = which_panel % cols_n
        column_slab = kernel_grid[:, :, slot_b, :]
        pivot_tile, pivot_rhs = (
            from_root(column_slab[slot_a], "row", root_r),
            from_root(current[slot_a], "row", root_r),
        )
        factor = jnp.linalg.cholesky(pivot_tile)
        inverse = jax.scipy.linalg.solve_triangular(factor, identity, lower=True)
        panel_tiles = jnp.einsum("ipq,sq->ips", column_slab, inverse, precision=HIGHEST)
        panel_tiles, inverse = (
            from_root(panel_tiles, "col", root_c),
            from_root(inverse, "col", root_c),
        )
        grouped_panel = panel_tiles.reshape(tile_cols, stride, tile_size, tile_size)
        chosen_panel = lax.dynamic_index_in_dim(grouped_panel, col_id // rows_n, 1, keepdims=False)
        panel_cols = from_root(chosen_panel, "row", col_id % rows_n)
        kernel_grid = kernel_grid - jnp.einsum(
            "ipk,jqk->ipjq", panel_tiles, panel_cols, precision=HIGHEST
        )
        current, answer = advance(
            current, panel_tiles, inverse, pivot_rhs, tile_of_row, which_panel
        )
        row_panels.append(panel_tiles)
        answers.append(answer)
    solved = current
    for which_panel in range(PANELS):
        solved = jnp.where(
            (tile_of_row == which_panel)[:, None, None], answers[which_panel][None], solved
        )
    trailing_mask = (tile_of_row >= PANELS)[:, None, None, None] & (tile_of_col >= PANELS)[
        None, None, :, None
    ]
    factored = jnp.where(trailing_mask, kernel_grid, 0.0)
    beneath = row_index[:, :, None, None] >= col_index[None, None, :, :]
    for which_panel in range(PANELS):
        pick = beneath & (tile_of_col == which_panel)[None, None, :, None]
        factored = jnp.where(pick, row_panels[which_panel][:, :, None, :], factored)
    return (factored[:, None, :, :, None, :], solved[:, None])


def solution(mesh):
    return jax.shard_map(
        per_device,
        mesh=mesh,
        in_specs=(P(None, "row", None, None), P(None, "row", None, "col")),
        out_specs=(P(None, "row", None, None, "col", None), P(None, "row", None, "col")),
        check_vma=False,
    )
```

profile of v0, /device:TPU:0, one launch (start us, length us, event | category | flops | bytes accessed | tf_op | source)
XLA Modules:
  0.0 532.4 jit_solution(501918577944356869)
XLA Ops:
  10.4 35.2 %all-reduce.10.cloned.1.call-done = f32[2,256,128]{2,1,0:T(8,128)} async-done(((f32[2,256,128]{2,1,0:T(8,128)}), f32[2,256,128]{2,1,0:T(8,128)}) %all-reduce.10.cloned.1.call-update) | async-done | bytes 262160 | tf_op jit(solution)/shard_map/psum | solution.py:16
  46.7 3.4 fusion.2
  51.6 31.5 %all-reduce.12.cloned.1.call-done = f32[256,256]{0,1:T(8,128)} async-done(((f32[256,256]{0,1:T(8,128)}), f32[256,256]{0,1:T(8,128)}) %all-reduce.12.cloned.1.call-update) | async-done | bytes 262160 | tf_op jit(solution)/shard_map/psum | solution.py:16
  85.2 11.7 %cholesky.130 = f32[128,128]{1,0:T(8,128)S(1)} custom-call(f32[128,128]{1,0:T(8,128)S(1)} %cholesky.194), custom_call_target="Cholesky" | custom-call | tf_op jit(solution)/shard_map/jit(cholesky)/cholesky | solution.py:72
  96.9 9.8 %custom-call.13 = f32[1,128,128]{1,2,0:T(8,128)S(1)} custom-call(f32[1,128,128]{2,1,0:T(8,128)S(1)} %get-tuple-element.54), custom_call_target="InvertDiagBlocksLowerTriangular" | custom-call | tf_op jit(solution)/shard_map/jit(cholesky)/cholesky | solution.py:72
  107.3 11.7 %cholesky.147 = f32[128,128]{1,0:T(8,128)S(1)} custom-call(f32[128,128]{1,0:T(8,128)S(1)} %convolution_subtract_fusion.6), custom_call_target="Cholesky" | custom-call | tf_op jit(solution)/shard_map/jit(cholesky)/cholesky | solution.py:72
  121.1 4.2 while.4
  125.4 19.7 %custom-call.14 = f32[2,128,128]{1,2,0:T(8,128)S(1)} custom-call(f32[2,128,128]{2,1,0:T(8,128)S(1)} %get-tuple-element.18), custom_call_target="InvertDiagBlocksLowerTriangular" | custom-call | tf_op jit(solution)/shard_map/jit(_solve_triangular)/triangular_solve | solution.py:73
  146.0 2.9 convolution_select_fusion.1
  148.9 78.1 %all-reduce.14.cloned.1.call-done = f32[4,256,256]{2,1,0:T(8,128)} async-done(((f32[4,256,256]{2,1,0:T(8,128)}), f32[4,256,256]{2,1,0:T(8,128)}) %all-reduce.14.cloned.1.call-update) | async-done | bytes 1048592 | tf_op jit(solution)/shard_map/psum | solution.py:16
  227.0 2.0 fusion.11
  229.1 33.1 %all-reduce.16.cloned.1.call-done = f32[2,256,256]{2,1,0:T(8,128)} async-done(((f32[2,256,256]{2,1,0:T(8,128)}), f32[2,256,256]{2,1,0:T(8,128)}) %all-reduce.16.cloned.1.call-update) | async-done | bytes 524304 | tf_op jit(solution)/shard_map/psum | solution.py:16
  262.2 3.6 convolution_subtract_fusion
  268.5 30.2 %all-reduce.18.cloned.1.call-done = f32[256,256]{0,1:T(8,128)} async-done(((f32[256,256]{0,1:T(8,128)}), f32[256,256]{0,1:T(8,128)}) %all-reduce.18.cloned.1.call-update) | async-done | bytes 262160 | tf_op jit(solution)/shard_map/psum | solution.py:16
  298.7 1.8 copy.23
  302.2 11.7 %cholesky.164 = f32[128,128]{1,0:T(8,128)S(1)} custom-call(f32[128,128]{1,0:T(8,128)S(1)} %cholesky.197), custom_call_target="Cholesky" | custom-call | tf_op jit(solution)/shard_map/jit(cholesky)/cholesky | solution.py:72
  314.7 10.4 %custom-call.15 = f32[1,128,128]{1,2,0:T(8,128)} custom-call(f32[1,128,128]{2,1,0:T(8,128)S(1)} %get-tuple-element.50), custom_call_target="InvertDiagBlocksLowerTriangular" | custom-call | tf_op jit(solution)/shard_map/jit(cholesky)/cholesky | solution.py:72
  325.8 1.7 constant_dynamic-update-slice_fusion
  328.6 11.7 %cholesky.181 = f32[128,128]{1,0:T(8,128)S(1)} custom-call(f32[128,128]{1,0:T(8,128)S(1)} %convolution_subtract_fusion.5), custom_call_target="Cholesky" | custom-call | tf_op jit(solution)/shard_map/jit(cholesky)/cholesky | solution.py:72
  343.7 5.9 %while.5 = (s32[]{:T(128)}, f32[256,256]{1,0:T(8,128)}, s32[2,2]{1,0:T(2,128)S(1)}, f32[2,128,128]{2,1,0:T(8,128)S(1)}, s32[]{:T(128)}) while((s32[]{:T(128)}, f32[256,256]{1,0:T(8,128)}, s32[2,2]{1,0:T(2,128)S(1)}, f32[2,128,128]{2,1,0:T(8,128)S(1)}, s32[]{:T(128)}) %tuple.73), condition=%wide.while_cond.clone, body=%wide.while_body.clone.sunk | while | flops 2 | bytes 131189 | solution.py:73
  344.5 2.3 bitcast_dynamic-update-slice_fusion.5
  347.4 2.2 bitcast_dynamic-update-slice_fusion.5
  350.3 20.5 %custom-call.16 = f32[2,128,128]{1,2,0:T(8,128)S(1)} custom-call(f32[2,128,128]{2,1,0:T(8,128)} %copy-done.6), custom_call_target="InvertDiagBlocksLowerTriangular" | custom-call | tf_op jit(solution)/shard_map/jit(_solve_triangular)/triangular_solve | solution.py:73
  373.2 2.8 convolution_select_fusion
  376.1 10.7 %psum.86 = f32[256,32]{0,1:T(8,128)S(1)} all-reduce(f32[256,32]{0,1:T(8,128)S(1)} %select_bitcast_fusion.3), channel_id=1, replica_groups=mesh['row'=4,'col'=8] {'row'}, use_global_device_ids=true, to_apply=%region_15.18 | all-reduce | flops 8192 | bytes 65536 | tf_op jit(solution)/shard_map/psum | solution.py:16
  388.2 77.7 %all-reduce.22.cloned.1.call-done = (f32[4,256,256]{2,1,0:T(8,128)}, f32[256,256]{1,0:T(8,128)}, f32[256,256]{1,0:T(8,128)}) async-done(((f32[4,256,256]{2,1,0:T(8,128)}, f32[256,256]{1,0:T(8,128)}, f32[256,256]{1,0:T(8,128)}), (f32[4,256,256]{2,1,0:T(8,128)}, f32[256,256]{1,0:T(8,128)}, f32[256,256]{1,0:T(8,128)})) %all-reduce.22.cloned.1.call-update) | async-done | bytes 1572880 | tf_op jit(solution)/shard_map/psum | solution.py:16
  467.3 2.3 fusion.4
  469.7 11.3 %psum.87 = f32[256,32]{0,1:T(8,128)S(1)} all-reduce(f32[256,32]{0,1:T(8,128)S(1)} %fusion.41), channel_id=1, replica_groups=mesh['row'=4,'col'=8] {'row'}, use_global_device_ids=true, to_apply=%region_16.19 | all-reduce | flops 8192 | bytes 65536 | tf_op jit(solution)/shard_map/psum | solution.py:16
  484.5 1.7 fusion.7
  486.2 27.5 %all-reduce.20.cloned.1.call-done = f32[2,256,256]{2,1,0:T(8,128)} async-done(((f32[2,256,256]{2,1,0:T(8,128)}), f32[2,256,256]{2,1,0:T(8,128)}) %all-reduce.20.cloned.1.call-update) | async-done | bytes 524304 | tf_op jit(solution)/shard_map/psum | solution.py:16
  513.7 5.5 %select_bitcast_fusion = f32[4,1,256,2,1,256]{2,5,3,0,4,1:T(8,128)} fusion(f32[4,256,2,256]{1,3,2,0:T(8,128)S(1)} %convolution_subtract_fusion, f32[4,256,256]{2,1,0:T(8,128)S(1)} %copy-done, f32[4,256,256]{1,2,0:T(8,128)} %copy.26, f32[4,256,256]{1,2,0:T(8,128)} %copy.25, s32[2,256]{1,0:T(2,128)S(1)} %iota_add_fusion.1, s32[4,256]{1,0:T(4,128)S(1)} %iota_add_fusion, ...), kind=kOutput, calls=%fused_computation.10 | convolution fusion | flops 1614282752 | bytes 7870476 | tf_op jit(solution)/shard_map/ipk,jqk->ipjq/dot_general | solution.py:82
  519.2 6.0 %copy.29 = f32[4,1,256,2,1,256]{5,4,3,2,1,0:T(1,128)} copy(f32[4,1,256,2,1,256]{2,5,3,0,4,1:T(8,128)} %select_bitcast_fusion) | data formatting | bytes 4194304
  (92 shorter events, 33.8 us)
Async XLA Ops:
  7.2 38.4 %all-reduce.10.cloned.1.call-start = ((), (), s32[]{:S(2)}) async-start(), calls=%async_computation | async-start | bytes 524288 | tf_op jit(solution)/shard_map/psum | solution.py:16
  8.9 74.1 %all-reduce.12.cloned.1.call-start = ((), (), s32[]{:S(2)}) async-start(), calls=%async_computation.1 | async-start | bytes 524288 | tf_op jit(solution)/shard_map/psum | solution.py:16
  50.2 95.8 %copy-start.2 = (f32[4,256,2,256]{1,3,2,0:T(8,128)}, f32[4,256,2,256]{1,3,2,0:T(8,128)S(1)}, u32[]{:S(2)}) copy-start(f32[4,256,2,256]{1,3,2,0:T(8,128)S(1)} %fusion.2) | copy-start | bytes 6291460
  51.0 176.0 %all-reduce.14.cloned.1.call-start = ((), (), s32[]{:S(2)}) async-start(), calls=%async_computation.2 | async-start | bytes 2097152 | tf_op jit(solution)/shard_map/psum | solution.py:16
  145.9 2.9 copy-start.3
  148.8 113.3 %all-reduce.16.cloned.1.call-start = ((), (), s32[]{:S(2)}) async-start(), calls=%async_computation.3 | async-start | bytes 1048576 | tf_op jit(solution)/shard_map/psum | solution.py:16
  227.0 35.2 %copy-start.1 = (f32[4,256,256]{2,1,0:T(8,128)S(1)}, f32[4,256,256]{2,1,0:T(8,128)}, u32[]{:S(2)}) copy-start(f32[4,256,256]{2,1,0:T(8,128)} %all-reduce.14.cloned.1.call-done) | copy-start | bytes 3145732
  229.0 69.7 %all-reduce.18.cloned.1.call-start = ((), (), s32[]{:S(2)}) async-start(), calls=%async_computation.4 | async-start | bytes 524288 | tf_op jit(solution)/shard_map/psum | solution.py:16
  266.5 199.4 %all-reduce.22.cloned.1.call-start = ((), (), s32[]{:S(2)}) async-start(), calls=%async_computation.6 | async-start | bytes 3145728 | tf_op jit(solution)/shard_map/psum | solution.py:16
  301.5 0.7 copy-start.4
  349.6 0.7 copy-start.6
  373.2 2.9 copy-start.5
  376.0 137.7 %all-reduce.20.cloned.1.call-start = ((), (), s32[]{:S(2)}) async-start(), calls=%async_computation.5 | async-start | bytes 1048576 | tf_op jit(solution)/shard_map/psum | solution.py:16
  466.0 15.0 %copy-start = (f32[4,256,256]{2,1,0:T(8,128)S(1)}, f32[4,256,256]{2,1,0:T(8,128)}, u32[]{:S(2)}) copy-start(f32[4,256,256]{2,1,0:T(8,128)} %get-tuple-element.40) | copy-start | bytes 3145732
Sparse Core Ops, SparseCore 0:
  10.9 34.6 all-reduce.9
  51.1 31.9 all-reduce.11
  149.0 77.9 all-reduce.13
  229.3 32.7 all-reduce.15
  266.7 31.9 all-reduce.17
  376.2 89.7 all-reduce.21
  482.0 31.7 all-reduce.19
where the time goes:
time: 536 us; the launch traced here: 532 us
  waiting for transfers between devices  313 us (58%)
  other arithmetic  124 us (23%)
  matrix products  30.8 us (6%)
  local copies, waits for them, and re-layouts  23.4 us (4%)
  blocking collectives  22 us (4%)
  between operations  17.3 us (3%)
    psum x7, waiting for transfers between devices, from_root(): return lax.psum(block, axis)  313 us
    another operation x13, other arithmetic, per_device(): factor = jnp.linalg.cholesky(pivot_tile)  69.9 us
    another operation x5, other arithmetic, per_device(): inverse = jax.scipy.linalg.solve_triangular(factor, identity, lower=True)  40.9 us
    psum x2, blocking collectives, from_root(): return lax.psum(block, axis)  22 us
  transfers between devices with their start and end apart: 7, of which 7 were waited for; matrix products, arithmetic and copies ran while one was open for 2% of the time, Pallas kernels for 0%

commit v1 on v0

v1 whole, which is shorter than its diff:
```python
import functools

import jax
import jax.numpy as jnp
from jax import lax
from jax.experimental import pallas as pl
from jax.experimental.pallas import tpu as pltpu
from jax.sharding import PartitionSpec as P

PANELS = 2
SCALE = 3.0
NUGGET = 1.0
HIGHEST = lax.Precision.HIGHEST
MESH = pl.DeviceIdType.MESH
F32 = jnp.float32
BF16 = jnp.bfloat16
NB = 64


def fetch_kernel(rows_n, cols_n, tile_cols, pts, prhs, piv, colp, rpiv, send, recv, local):
    row_id = lax.axis_index("row")
    col_id = lax.axis_index("col")
    stride = cols_n // rows_n

    barrier = pltpu.get_barrier_semaphore()
    for step in range(1, rows_n):
        other = lax.rem(row_id + step, rows_n)
        pl.semaphore_signal(barrier, inc=1, device_id={"row": other}, device_id_type=MESH)
    pl.semaphore_wait(barrier, rows_n - 1)

    jobs = []
    for k in range(PANELS):
        jobs.append((k % rows_n, pts.at[k // rows_n], piv.at[k]))
        jobs.append((k % rows_n, prhs.at[k // rows_n], rpiv.at[k]))
    for c2 in range(tile_cols):
        slot = c2 * stride + col_id // rows_n
        jobs.append((lax.rem(col_id, rows_n), pts.at[slot], colp.at[c2]))

    def remote(number, step):
        _, src, dst = jobs[number]
        return pltpu.make_async_remote_copy(
            src_ref=src,
            dst_ref=dst,
            send_sem=send.at[number, step - 1],
            recv_sem=recv.at[number],
            device_id={"row": lax.rem(row_id + step, rows_n)},
            device_id_type=MESH,
        )

    for number, (owner, src, dst) in enumerate(jobs):

        @pl.when(row_id == owner)
        def _(number=number, src=src, dst=dst):
            for step in range(1, rows_n):
                remote(number, step).start()
            pltpu.make_async_copy(src, dst, local.at[number]).start()

    for number, (owner, src, dst) in enumerate(jobs):

        @pl.when(row_id == owner)
        def _(number=number, src=src, dst=dst):
            for step in range(1, rows_n):
                remote(number, step).wait_send()
            pltpu.make_async_copy(src, dst, local.at[number]).wait()

        @pl.when(row_id != owner)
        def _(number=number):
            remote(number, 1).wait_recv()


def split(x):
    hi = x.astype(BF16)
    return hi, (x - hi.astype(F32)).astype(BF16)


def nt(a, b):
    return lax.dot_general(a, b, (((1,), (1,)), ((), ())), preferred_element_type=F32)


def nt3(a, b):
    return nt(a[0], b[0]) + (nt(a[0], b[1]) + nt(a[1], b[0]))


def squared_exp(a, b, b_sq):
    a_sq = jnp.sum(a * a, axis=1, keepdims=True)
    inner = nt3(split(a), split(b))
    return jnp.exp((-SCALE / a.shape[1]) * (a_sq + b_sq - 2.0 * inner))


def row_squares(b):
    ones = jnp.ones((8, b.shape[1]), F32)
    return lax.dot_general(
        ones, b * b, (((1,), (1,)), ((), ())), precision=HIGHEST, preferred_element_type=F32
    )[:1]


def base_inverse(block):
    lane = lax.broadcasted_iota(jnp.int32, (8, 2 * NB), 1)
    sub = lax.broadcasted_iota(jnp.int32, (8, 2 * NB), 0)
    eye = (
        lax.broadcasted_iota(jnp.int32, (NB, NB), 0) == lax.broadcasted_iota(jnp.int32, (NB, NB), 1)
    ).astype(F32)
    wide = jnp.concatenate([block, eye], axis=1)
    v = [wide[8 * q : 8 * q + 8] for q in range(NB // 8)]
    for j in range(NB):
        q0, s = divmod(j, 8)
        row = v[q0][s : s + 1]
        scaled = row * (1.0 / row[:, j : j + 1])
        for q in range(q0, NB // 8):
            col = v[q][:, j : j + 1]
            if q == q0:
                if s == 7:
                    continue
                col = jnp.where(sub[:, :1] > s, col, 0.0)
            v[q] = v[q] - col * scaled
    out = []
    for q in range(NB // 8):
        diag = jnp.sum(jnp.where(lane == sub + 8 * q, v[q], 0.0), axis=1, keepdims=True)
        out.append(v[q] * lax.rsqrt(diag))
    return jnp.concatenate(out, axis=0)[:, NB:]


def inverse_factor(w, h):
    size = h.shape[0]
    for j0 in range(0, size, NB):
        j1 = j0 + NB
        inv = base_inverse(w[j0:j1, j0:j1])
        rows = jnp.dot(inv, w[j0:j1, :], precision=HIGHEST, preferred_element_type=F32)
        h[j0:j1, :] = rows[:, size:]
        if j1 < size:
            panel = lax.dot_general(
                w[j1:, j0:j1], inv, (((1,), (1,)), ((), ())), precision=HIGHEST, preferred_element_type=F32
            )
            w[j1:, :] = w[j1:, :] - jnp.dot(
                panel, rows, precision=HIGHEST, preferred_element_type=F32
            )


def main_kernel(
    rows_n, cols_n, pts, piv, colp, rhs, rpiv, out, solved, w, h0, h1, l10, lf, lh, ll, yh, yl
):
    row_id = lax.axis_index("row")
    col_id = lax.axis_index("col")
    tile_rows, size, _ = pts.shape
    tile_cols = colp.shape[0]
    row_in = lax.broadcasted_iota(jnp.int32, (size, size), 0)
    col_in = lax.broadcasted_iota(jnp.int32, (size, size), 1)
    eye = (row_in == col_in).astype(F32)
    lower = row_in >= col_in
    x0, x1 = piv[0], piv[1]
    sq0, sq1 = row_squares(x0), row_squares(x1)

    w[:, :size] = squared_exp(x0, x0, sq0) + NUGGET * eye
    w[:, size:] = eye
    inverse_factor(w, h0)
    h0s = split(h0[...])
    l10[...] = nt3(split(squared_exp(x1, x0, sq0)), h0s)
    l10s = split(l10[...])
    w[:, :size] = squared_exp(x1, x1, sq1) + NUGGET * eye - nt3(l10s, l10s)
    w[:, size:] = eye
    inverse_factor(w, h1)
    h1s = split(h1[...])

    y0 = nt3(split(rpiv[0]), h0s)
    y1 = nt3(split(rpiv[1] - nt3(split(y0), l10s)), h1s)
    yh[:, :size], yl[:, :size] = split(y0)
    yh[:, size:], yl[:, size:] = split(y1)

    def panels_of(x, tile):
        k0 = squared_exp(x, x0, sq0) + jnp.where(tile == 0, NUGGET, 0.0) * eye
        l0 = nt3(split(k0), h0s)
        l0 = jnp.where((tile != 0) | lower, l0, 0.0)
        k1 = squared_exp(x, x1, sq1) + jnp.where(tile == 1, NUGGET, 0.0) * eye
        l1 = nt3(split(k1 - nt3(split(l0), l10s)), h1s)
        l1 = jnp.where((tile > 1) | (lower & (tile == 1)), l1, 0.0)
        return l0, l1

    @pl.loop(0, tile_cols)
    def _(c2):
        l0, l1 = panels_of(colp[c2], c2 * cols_n + col_id)
        lh[c2, :, :size], ll[c2, :, :size] = split(l0)
        lh[c2, :, size:], ll[c2, :, size:] = split(l1)

    @pl.loop(0, tile_rows)
    def _(a):
        tile = a * rows_n + row_id
        x = pts[a]
        l0, l1 = panels_of(x, tile)
        lf[:, :size] = l0
        lf[:, size:] = l1
        ls = split(lf[...])
        rest = rhs[a] - nt3((yh[...], yl[...]), ls)
        solved[a] = jnp.where(tile == 0, y0, jnp.where(tile == 1, y1, rest))
        for c2 in range(tile_cols):
            tile_c = c2 * cols_n + col_id
            xc = colp[c2]
            k = squared_exp(x, xc, row_squares(xc)) + jnp.where(tile == tile_c, NUGGET, 0.0) * eye
            s = k - nt3(ls, (lh[c2], ll[c2]))
            s = jnp.where(tile >= PANELS, s, 0.0)
            if c2 == 0:
                s = jnp.where(tile_c == 0, lf[:, :size], jnp.where(tile_c == 1, lf[:, size:], s))
            for half in range(size // 128):
                out[a, pl.ds(c2 * (size // 128) + half, size, stride=tile_cols * size // 128), :] = s[
                    :, half * 128 : half * 128 + 128
                ]


def per_device(points, rhs):
    rows_n = lax.axis_size("row")
    cols_n = lax.axis_size("col")
    tile_rows, _, size, feat = points.shape
    width = rhs.shape[-1]
    tile_cols = tile_rows * rows_n // cols_n
    pts = points[:, 0]
    right = rhs[:, 0].swapaxes(1, 2)
    jobs = 2 * PANELS + tile_cols
    any_spec = pl.BlockSpec(memory_space=pl.ANY)
    vmem = pl.BlockSpec(memory_space=pltpu.VMEM)
    piv, colp, rpiv = pl.pallas_call(
        functools.partial(fetch_kernel, rows_n, cols_n, tile_cols),
        out_shape=(
            jax.ShapeDtypeStruct((PANELS, size, feat), F32),
            jax.ShapeDtypeStruct((tile_cols, size, feat), F32),
            jax.ShapeDtypeStruct((PANELS, width, size), F32),
        ),
        in_specs=[any_spec] * 2,
        out_specs=(any_spec,) * 3,
        scratch_shapes=[
            pltpu.SemaphoreType.DMA((jobs, rows_n - 1)),
            pltpu.SemaphoreType.DMA((jobs,)),
            pltpu.SemaphoreType.DMA((jobs,)),
        ],
        compiler_params=pltpu.CompilerParams(collective_id=0, has_side_effects=True),
        name="fetch",
    )(pts, right)
    factored, solved = pl.pallas_call(
        functools.partial(main_kernel, rows_n, cols_n),
        out_shape=(
            jax.ShapeDtypeStruct((tile_rows, size * tile_cols * size // 128, 128), F32),
            jax.ShapeDtypeStruct((tile_rows, width, size), F32),
        ),
        in_specs=[vmem] * 5,
        out_specs=(vmem,) * 2,
        scratch_shapes=[
            pltpu.VMEM((size, 2 * size), F32),
            pltpu.VMEM((size, size), F32),
            pltpu.VMEM((size, size), F32),
            pltpu.VMEM((size, size), F32),
            pltpu.VMEM((size, 2 * size), F32),
            pltpu.VMEM((tile_cols, size, 2 * size), BF16),
            pltpu.VMEM((tile_cols, size, 2 * size), BF16),
            pltpu.VMEM((width, 2 * size), BF16),
            pltpu.VMEM((width, 2 * size), BF16),
        ],
        compiler_params=pltpu.CompilerParams(vmem_limit_bytes=48 * 1024 * 1024),
        name="panels",
    )(pts, piv, colp, right, rpiv)
    factored = factored.reshape(tile_rows, 1, size, tile_cols, 1, size)
    return factored, solved.swapaxes(1, 2)[:, None]


def solution(mesh):
    return jax.shard_map(
        per_device,
        mesh=mesh,
        in_specs=(P(None, "row", None, None), P(None, "row", None, "col")),
        out_specs=(P(None, "row", None, None, "col", None), P(None, "row", None, "col")),
        check_vma=False,
    )
```

time: 536 us -> 85.1 us (0.16)
  waiting for transfers between devices: 313 us -> 0 us
  other arithmetic: 124 us -> 0 us
  Pallas kernels: 0 us -> 79.5 us
  matrix products: 30.8 us -> 0 us
  blocking collectives: 22 us -> 0 us
  local copies, waits for them, and re-layouts: 23.4 us -> 4.68 us
  between operations: 17.3 us -> 0.65 us
    psum x7 -> x0, waiting for transfers between devices: 313 us -> none  [from_root(): return lax.psum(block, axis)]
    another operation x18 -> x0, other arithmetic: 111 us -> none  [the longest x13 69.9 us: per_device(): factor = jnp.linalg.cholesky(pivot_tile)]
    pallas_call x0 -> x2, Pallas kernels: none -> 79.5 us  [the longest x1 62.2 us: per_device(): pl.pallas_call(functools.partial(main_kernel, rows_n, cols_n), out_shape=...]
    dot_general x9 -> x0, matrix products: 24.9 us -> none  [the longest x2 9.13 us: per_device(): jnp.einsum('ipk,jqk->ipjq', panel_tiles, panel_cols, precision=HIGHEST)]
    psum x2 -> x0, blocking collectives: 22 us -> none  [from_root(): return lax.psum(block, axis)]
    another operation x19 -> x0, local copies, waits for them, and re-layouts: 10.5 us -> none  [the longest x15 9.74 us: per_device(): inverse = jax.scipy.linalg.solve_triangular(factor, identity, lower=True)]
    select_n x9 -> x0, other arithmetic: 8.38 us -> none  [from_root(): jnp.where(lax.axis_index(axis) == owner, block, jnp.zeros_like(block))]
    another operation x10 -> x0, matrix products: 5.87 us -> none  [the longest x4 3.28 us: per_device(): factor = jnp.linalg.cholesky(pivot_tile)]
  transfers between devices with their start and end apart: 7 -> 0, of which waited for: 7 -> 0; matrix products, arithmetic and copies ran while one was open for 2% -> 0% of each run, Pallas kernels for 0% -> 0%
where the time goes in v1:
time: 85.1 us; the launch traced here: 84.8 us
  Pallas kernels  79.5 us (93%)
  local copies, waits for them, and re-layouts  4.68 us (5%)
    pallas_call x1, Pallas kernels, per_device(): pl.pallas_call(functools.partial(main_kernel, rows_n, cols_n), out_shape=...  62.2 us
    pallas_call x1, Pallas kernels, per_device(): pl.pallas_call(functools.partial(fetch_kernel, rows_n, cols_n, tile_cols)...  17.3 us
    unnamed x10, local copies, waits for them, and re-layouts  4.68 us

profile of v1, /device:TPU:0, one launch (start us, length us, event | category | flops | bytes accessed | tf_op | source)
XLA Modules:
  0.0 84.8 jit_solution(17477861844272646107)
XLA Ops:
  0.6 17.3 %fetch.1 = (f32[2,256,128]{2,1,0:T(8,128)}, f32[2,256,128]{2,1,0:T(8,128)}, f32[2,32,256]{2,1,0:T(8,128)}) custom-call(f32[4,256,128]{2,1,0:T(8,128)} %bitcast.10, f32[4,32,256]{2,1,0:T(8,128)} %bitcast.12), custom_call_target="tpu_custom_call" | custom-call | tf_op jit(solution)/shard_map/fetch/pallas_call | solution.py:219
  17.9 0.0 copy-start
  17.9 1.0 %copy-done = f32[4,1,256,128]{3,2,1,0:T(8,128)S(1)} copy-done((f32[4,1,256,128]{3,2,1,0:T(8,128)S(1)}, f32[4,1,256,128]{3,2,1,0:T(8,128)}, u32[]{:S(2)}) %copy-start) | copy-done | bytes 524312
  19.0 0.0 copy-start.1
  19.0 0.9 %copy-done.1 = f32[4,1,256,32]{2,3,1,0:T(8,128)S(1)} copy-done((f32[4,1,256,32]{2,3,1,0:T(8,128)S(1)}, f32[4,1,256,32]{2,3,1,0:T(8,128)}, u32[]{:S(2)}) %copy-start.1) | copy-done | bytes 131096
  19.9 0.0 copy-start.2
  19.9 0.9 %copy-done.2 = f32[2,256,128]{2,1,0:T(8,128)S(1)} copy-done((f32[2,256,128]{2,1,0:T(8,128)S(1)}, f32[2,256,128]{2,1,0:T(8,128)}, u32[]{:S(2)}) %copy-start.2) | copy-done | bytes 262168
  20.8 0.0 copy-start.3
  20.8 0.9 %copy-done.3 = f32[2,256,128]{2,1,0:T(8,128)S(1)} copy-done((f32[2,256,128]{2,1,0:T(8,128)S(1)}, f32[2,256,128]{2,1,0:T(8,128)}, u32[]{:S(2)}) %copy-start.3) | copy-done | bytes 262168
  21.8 0.0 copy-start.4
  21.8 0.8 copy-done.4
  22.6 62.2 %panels.1 = (f32[4,1024,128]{2,1,0:T(8,128)}, f32[4,32,256]{2,1,0:T(8,128)}) custom-call(f32[4,256,128]{2,1,0:T(8,128)S(1)} %bitcast.11, f32[2,256,128]{2,1,0:T(8,128)S(1)} %copy-done.2, f32[2,256,128]{2,1,0:T(8,128)S(1)} %copy-done.3, f32[4,32,256]{2,1,0:T(8,128)S(1)} %bitcast.13, f32[2,32,256]{2,1,0:T(8,128)S(1)} %copy-done.4), custom_call_target="tpu_custom_call" | custom-call | tf_op jit(solution)/shard_map/panels/pallas_call | solution.py:236
Async XLA Ops:
  17.9 1.0 %copy-start = (f32[4,1,256,128]{3,2,1,0:T(8,128)S(1)}, f32[4,1,256,128]{3,2,1,0:T(8,128)}, u32[]{:S(2)}) copy-start(f32[4,1,256,128]{3,2,1,0:T(8,128)} %param.2) | copy-start | bytes 1572868
  19.0 0.9 %copy-start.1 = (f32[4,1,256,32]{2,3,1,0:T(8,128)S(1)}, f32[4,1,256,32]{2,3,1,0:T(8,128)}, u32[]{:S(2)}) copy-start(f32[4,1,256,32]{2,3,1,0:T(8,128)} %param.3) | copy-start | bytes 393220
  19.9 0.9 %copy-start.2 = (f32[2,256,128]{2,1,0:T(8,128)S(1)}, f32[2,256,128]{2,1,0:T(8,128)}, u32[]{:S(2)}) copy-start(f32[2,256,128]{2,1,0:T(8,128)} %get-tuple-element.7.piv) | copy-start | bytes 786436
  20.8 0.9 %copy-start.3 = (f32[2,256,128]{2,1,0:T(8,128)S(1)}, f32[2,256,128]{2,1,0:T(8,128)}, u32[]{:S(2)}) copy-start(f32[2,256,128]{2,1,0:T(8,128)} %get-tuple-element.8.colp) | copy-start | bytes 786436
  21.8 0.8 copy-start.4

commit v2 on v1

--- a/solution.py
+++ b/solution.py
@@ -36,36 +36,66 @@
         slot = c2 * stride + col_id // rows_n
         jobs.append((lax.rem(col_id, rows_n), pts.at[slot], colp.at[c2]))
 
-    def remote(number, step):
+    chips = rows_n // 2
+    chip, core = row_id // 2, lax.rem(row_id, 2)
+    sibling = row_id + 1 - 2 * core
+
+    def half_of(ref, half):
+        height = ref.shape[0] // 2
+        return ref.at[pl.ds(pl.multiple_of(half * height, height), height)]
+
+    def remote(number, half, dest, slot, relay=False):
         _, src, dst = jobs[number]
         return pltpu.make_async_remote_copy(
-            src_ref=src,
-            dst_ref=dst,
-            send_sem=send.at[number, step - 1],
-            recv_sem=recv.at[number],
-            device_id={"row": lax.rem(row_id + step, rows_n)},
+            src_ref=half_of(dst if relay else src, half),
+            dst_ref=half_of(dst, half),
+            send_sem=send.at[number, slot],
+            recv_sem=recv.at[number, half],
+            device_id={"row": dest},
             device_id_type=MESH,
         )
 
+    def sends(number):
+        out = []
+        for step in range(1, chips):
+            for half in range(2):
+                dest = 2 * lax.rem(chip + step, chips) + half
+                out.append(remote(number, half, dest, 2 * step + half))
+        return out + [remote(number, half, sibling, half) for half in range(2)]
+
     for number, (owner, src, dst) in enumerate(jobs):
 
         @pl.when(row_id == owner)
         def _(number=number, src=src, dst=dst):
-            for step in range(1, rows_n):
-                remote(number, step).start()
+            for copy in sends(number):
+                copy.start()
             pltpu.make_async_copy(src, dst, local.at[number]).start()
+
+    for number, (owner, src, dst) in enumerate(jobs):
+
+        @pl.when(chip != owner // 2)
+        def _(number=number):
+            relay = remote(number, core, sibling, 0, relay=True)
+            relay.wait_recv()
+            relay.start()
 
     for number, (owner, src, dst) in enumerate(jobs):
 
         @pl.when(row_id == owner)
         def _(number=number, src=src, dst=dst):
-            for step in range(1, rows_n):
-                remote(number, step).wait_send()
+            for copy in sends(number):
+                copy.wait_send()
             pltpu.make_async_copy(src, dst, local.at[number]).wait()
 
-        @pl.when(row_id != owner)
+        @pl.when(sibling == owner)
         def _(number=number):
-            remote(number, 1).wait_recv()
+            for half in range(2):
+                remote(number, half, sibling, half).wait_recv()
+
+        @pl.when(chip != owner // 2)
+        def _(number=number):
+            remote(number, core, sibling, 0, relay=True).wait_send()
+            remote(number, 1 - core, sibling, 0, relay=True).wait_recv()
 
 
 def split(x):
@@ -94,37 +124,34 @@
     )[:1]
 
 
-def base_inverse(block):
-    lane = lax.broadcasted_iota(jnp.int32, (8, 2 * NB), 1)
-    sub = lax.broadcasted_iota(jnp.int32, (8, 2 * NB), 0)
+def base_inverse(block, base):
     eye = (
         lax.broadcasted_iota(jnp.int32, (NB, NB), 0) == lax.broadcasted_iota(jnp.int32, (NB, NB), 1)
     ).astype(F32)
     wide = jnp.concatenate([block, eye], axis=1)
     v = [wide[8 * q : 8 * q + 8] for q in range(NB // 8)]
-    for j in range(NB):
+    for j in range(0, NB, 2):
         q0, s = divmod(j, 8)
-        row = v[q0][s : s + 1]
-        scaled = row * (1.0 / row[:, j : j + 1])
-        for q in range(q0, NB // 8):
-            col = v[q][:, j : j + 1]
-            if q == q0:
-                if s == 7:
-                    continue
-                col = jnp.where(sub[:, :1] > s, col, 0.0)
-            v[q] = v[q] - col * scaled
-    out = []
-    for q in range(NB // 8):
-        diag = jnp.sum(jnp.where(lane == sub + 8 * q, v[q], 0.0), axis=1, keepdims=True)
-        out.append(v[q] * lax.rsqrt(diag))
-    return jnp.concatenate(out, axis=0)[:, NB:]
-
-
-def inverse_factor(w, h):
+        r0, r1 = v[q0][s : s + 1], v[q0][s + 1 : s + 2]
+        a, b = r0[:, j : j + 1], r0[:, j + 1 : j + 2]
+        b1, c = r1[:, j : j + 1], r1[:, j + 1 : j + 2]
+        det = a * c - b * b1
+        inv_det = 1.0 / det
+        s0 = (c * r0 - b * r1) * inv_det
+        s1 = (a * r1 - b1 * r0) * inv_det
+        rs = lax.rsqrt(a)
+        base[j : j + 1, :] = r0 * rs
+        base[j + 1 : j + 2, :] = (a * r1 - b1 * r0) * (lax.rsqrt(det) * rs)
+        for q in range(q0 if s < 6 else q0 + 1, NB // 8):
+            v[q] = v[q] - v[q][:, j : j + 1] * s0 - v[q][:, j + 1 : j + 2] * s1
+    return base[:, NB:]
+
+
+def inverse_factor(w, h, base):
     size = h.shape[0]
     for j0 in range(0, size, NB):
         j1 = j0 + NB
-        inv = base_inverse(w[j0:j1, j0:j1])
+        inv = base_inverse(w[j0:j1, j0:j1], base)
         rows = jnp.dot(inv, w[j0:j1, :], precision=HIGHEST, preferred_element_type=F32)
         h[j0:j1, :] = rows[:, size:]
         if j1 < size:
@@ -137,8 +164,18 @@
 
 
 def main_kernel(
-    rows_n, cols_n, pts, piv, colp, rhs, rpiv, out, solved, w, h0, h1, l10, lf, lh, ll, yh, yl
+    rows_n, cols_n, hpts, hpiv, hcolp, hrhs, hrpiv, out, solved,
+    pts, piv, colp, rhs, rpiv, sems, base, w, h0, h1, l10, lf, lh, ll, yh, yl,
 ):
+    copies = [
+        pltpu.make_async_copy(src, dst, sems.at[n])
+        for n, (src, dst) in enumerate(
+            ((hpiv, piv), (hrpiv, rpiv), (hcolp, colp), (hpts, pts), (hrhs, rhs))
+        )
+    ]
+    for copy in copies:
+        copy.start()
+    copies[0].wait()
     row_id = lax.axis_index("row")
     col_id = lax.axis_index("col")
     tile_rows, size, _ = pts.shape
@@ -152,15 +189,17 @@
 
     w[:, :size] = squared_exp(x0, x0, sq0) + NUGGET * eye
     w[:, size:] = eye
-    inverse_factor(w, h0)
+    inverse_factor(w, h0, base)
     h0s = split(h0[...])
     l10[...] = nt3(split(squared_exp(x1, x0, sq0)), h0s)
     l10s = split(l10[...])
     w[:, :size] = squared_exp(x1, x1, sq1) + NUGGET * eye - nt3(l10s, l10s)
     w[:, size:] = eye
-    inverse_factor(w, h1)
+    inverse_factor(w, h1, base)
     h1s = split(h1[...])
 
+    for copy in copies[1:]:
+        copy.wait()
     y0 = nt3(split(rpiv[0]), h0s)
     y1 = nt3(split(rpiv[1] - nt3(split(y0), l10s)), h1s)
     yh[:, :size], yl[:, :size] = split(y0)
@@ -226,8 +265,8 @@
         in_specs=[any_spec] * 2,
         out_specs=(any_spec,) * 3,
         scratch_shapes=[
-            pltpu.SemaphoreType.DMA((jobs, rows_n - 1)),
-            pltpu.SemaphoreType.DMA((jobs,)),
+            pltpu.SemaphoreType.DMA((jobs, rows_n)),
+            pltpu.SemaphoreType.DMA((jobs, 2)),
             pltpu.SemaphoreType.DMA((jobs,)),
         ],
         compiler_params=pltpu.CompilerParams(collective_id=0, has_side_effects=True),
@@ -239,9 +278,16 @@
             jax.ShapeDtypeStruct((tile_rows, size * tile_cols * size // 128, 128), F32),
             jax.ShapeDtypeStruct((tile_rows, width, size), F32),
         ),
-        in_specs=[vmem] * 5,
+        in_specs=[any_spec] * 5,
         out_specs=(vmem,) * 2,
         scratch_shapes=[
+            pltpu.VMEM(pts.shape, F32),
+            pltpu.VMEM(piv.shape, F32),
+            pltpu.VMEM(colp.shape, F32),
+            pltpu.VMEM(right.shape, F32),
+            pltpu.VMEM(rpiv.shape, F32),
+            pltpu.SemaphoreType.DMA((5,)),
+            pltpu.VMEM((NB, 2 * NB), F32),
             pltpu.VMEM((size, 2 * size), F32),
             pltpu.VMEM((size, size), F32),
             pltpu.VMEM((size, size), F32),

time: 85.1 us -> 99.8 us (1.17)
  Pallas kernels: 79.5 us -> 94.1 us
    pallas_call x1, Pallas kernels: 62.2 us -> 76.7 us  [per_device(): pl.pallas_call(functools.partial(main_kernel, rows_n, cols_n), out_shape=...]
where the time goes in v2:
time: 99.8 us; the launch traced here: 99.6 us
  Pallas kernels  94.1 us (94%)
  local copies, waits for them, and re-layouts  4.68 us (5%)
    pallas_call x1, Pallas kernels, per_device(): pl.pallas_call(functools.partial(main_kernel, rows_n, cols_n), out_shape=...  76.7 us
    pallas_call x1, Pallas kernels, per_device(): pl.pallas_call(functools.partial(fetch_kernel, rows_n, cols_n, tile_cols)...  17.4 us
    unnamed x10, local copies, waits for them, and re-layouts  4.68 us

profile of v2, /device:TPU:0, one launch (start us, length us, event | category | flops | bytes accessed | tf_op | source)
XLA Modules:
  0.0 99.6 jit_solution(4447409435145218214)
XLA Ops:
  0.6 17.4 %fetch.1 = (f32[2,256,128]{2,1,0:T(8,128)}, f32[2,256,128]{2,1,0:T(8,128)}, f32[2,32,256]{2,1,0:T(8,128)}) custom-call(f32[4,256,128]{2,1,0:T(8,128)} %bitcast.10, f32[4,32,256]{2,1,0:T(8,128)} %bitcast.12), custom_call_target="tpu_custom_call" | custom-call | tf_op jit(solution)/shard_map/fetch/pallas_call | solution.py:258
  18.0 0.0 copy-start
  18.0 1.0 %copy-done = f32[4,1,256,128]{3,2,1,0:T(8,128)S(1)} copy-done((f32[4,1,256,128]{3,2,1,0:T(8,128)S(1)}, f32[4,1,256,128]{3,2,1,0:T(8,128)}, u32[]{:S(2)}) %copy-start) | copy-done | bytes 524312
  19.1 0.0 copy-start.1
  19.1 0.9 copy-done.1
  20.0 0.0 copy-start.2
  20.0 0.9 copy-done.2
  20.9 0.0 copy-start.3
  20.9 0.9 copy-done.3
  21.9 0.0 copy-start.4
  21.9 0.8 copy-done.4
  22.7 76.7 %panels.1 = (f32[4,1024,128]{2,1,0:T(8,128)}, f32[4,32,256]{2,1,0:T(8,128)}) custom-call(f32[4,256,128]{2,1,0:T(8,128)S(1)} %bitcast.11, f32[2,256,128]{2,1,0:T(8,128)S(1)} %copy-done.2, f32[2,256,128]{2,1,0:T(8,128)S(1)} %copy-done.3, f32[4,32,256]{2,1,0:T(8,128)S(1)} %bitcast.13, f32[2,32,256]{2,1,0:T(8,128)S(1)} %copy-done.4), custom_call_target="tpu_custom_call" | custom-call | tf_op jit(solution)/shard_map/panels/pallas_call | solution.py:275
Async XLA Ops:
  18.0 1.0 %copy-start = (f32[4,1,256,128]{3,2,1,0:T(8,128)S(1)}, f32[4,1,256,128]{3,2,1,0:T(8,128)}, u32[]{:S(2)}) copy-start(f32[4,1,256,128]{3,2,1,0:T(8,128)} %param.2) | copy-start | bytes 1572868
  19.1 0.9 copy-start.1
  20.0 0.9 copy-start.2
  20.9 0.9 copy-start.3
  21.9 0.8 copy-start.4

commit v3 on v2

--- a/solution.py
+++ b/solution.py
@@ -14,7 +14,7 @@
 MESH = pl.DeviceIdType.MESH
 F32 = jnp.float32
 BF16 = jnp.bfloat16
-NB = 64
+NB = 128
 
 
 def fetch_kernel(rows_n, cols_n, tile_cols, pts, prhs, piv, colp, rpiv, send, recv, local):
@@ -124,6 +124,10 @@
     )[:1]
 
 
+def spread(column):
+    return jnp.broadcast_to(column, (column.shape[0], 2 * NB))
+
+
 def base_inverse(block, base):
     eye = (
         lax.broadcasted_iota(jnp.int32, (NB, NB), 0) == lax.broadcasted_iota(jnp.int32, (NB, NB), 1)
@@ -132,18 +136,21 @@
     v = [wide[8 * q : 8 * q + 8] for q in range(NB // 8)]
     for j in range(0, NB, 2):
         q0, s = divmod(j, 8)
+        first = [spread(v[q][:, j : j + 1]) for q in range(q0, NB // 8)]
+        second = [spread(v[q][:, j + 1 : j + 2]) for q in range(q0, NB // 8)]
         r0, r1 = v[q0][s : s + 1], v[q0][s + 1 : s + 2]
-        a, b = r0[:, j : j + 1], r0[:, j + 1 : j + 2]
-        b1, c = r1[:, j : j + 1], r1[:, j + 1 : j + 2]
+        a, b = first[0][s : s + 1], second[0][s : s + 1]
+        b1, c = first[0][s + 1 : s + 2], second[0][s + 1 : s + 2]
         det = a * c - b * b1
         inv_det = 1.0 / det
+        e1 = a * r1 - b1 * r0
         s0 = (c * r0 - b * r1) * inv_det
-        s1 = (a * r1 - b1 * r0) * inv_det
+        s1 = e1 * inv_det
         rs = lax.rsqrt(a)
         base[j : j + 1, :] = r0 * rs
-        base[j + 1 : j + 2, :] = (a * r1 - b1 * r0) * (lax.rsqrt(det) * rs)
+        base[j + 1 : j + 2, :] = e1 * (lax.rsqrt(det) * rs)
         for q in range(q0 if s < 6 else q0 + 1, NB // 8):
-            v[q] = v[q] - v[q][:, j : j + 1] * s0 - v[q][:, j + 1 : j + 2] * s1
+            v[q] = v[q] - first[q - q0] * s0 - second[q - q0] * s1
     return base[:, NB:]
 
 
@@ -278,7 +285,7 @@
             jax.ShapeDtypeStruct((tile_rows, size * tile_cols * size // 128, 128), F32),
             jax.ShapeDtypeStruct((tile_rows, width, size), F32),
         ),
-        in_specs=[any_spec] * 5,
+        in_specs=[pl.BlockSpec(memory_space=pltpu.HBM)] * 5,
         out_specs=(vmem,) * 2,
         scratch_shapes=[
             pltpu.VMEM(pts.shape, F32),

time: 99.8 us -> 64.4 us (0.65)
  Pallas kernels: 94.1 us -> 58.7 us
    pallas_call x1, Pallas kernels: 76.7 us -> 41.3 us  [per_device(): pl.pallas_call(functools.partial(main_kernel, rows_n, cols_n), out_shape=...]
where the time goes in v3:
time: 64.4 us; the launch traced here: 64.1 us
  Pallas kernels  58.7 us (91%)
  local copies, waits for them, and re-layouts  4.68 us (7%)
  between operations  0.81 us (1%)
    pallas_call x1, Pallas kernels, per_device(): pl.pallas_call(functools.partial(main_kernel, rows_n, cols_n), out_shape=...  41.3 us
    pallas_call x1, Pallas kernels, per_device(): pl.pallas_call(functools.partial(fetch_kernel, rows_n, cols_n, tile_cols)...  17.4 us
    unnamed x10, local copies, waits for them, and re-layouts  4.68 us

profile of v3, /device:TPU:0, one launch (start us, length us, event | category | flops | bytes accessed | tf_op | source)
XLA Modules:
  0.0 64.1 jit_solution(5989724823045156833)
XLA Ops:
  0.6 17.4 %fetch.1 = (f32[2,256,128]{2,1,0:T(8,128)}, f32[2,256,128]{2,1,0:T(8,128)}, f32[2,32,256]{2,1,0:T(8,128)}) custom-call(f32[4,256,128]{2,1,0:T(8,128)} %bitcast.10, f32[4,32,256]{2,1,0:T(8,128)} %bitcast.12), custom_call_target="tpu_custom_call" | custom-call | tf_op jit(solution)/shard_map/fetch/pallas_call | solution.py:265
  18.0 0.0 copy-start
  18.0 1.0 %copy-done = f32[4,1,256,128]{3,2,1,0:T(8,128)S(1)} copy-done((f32[4,1,256,128]{3,2,1,0:T(8,128)S(1)}, f32[4,1,256,128]{3,2,1,0:T(8,128)}, u32[]{:S(2)}) %copy-start) | copy-done | bytes 524312
  19.1 0.0 copy-start.1
  19.1 0.9 %copy-done.1 = f32[4,1,256,32]{2,3,1,0:T(8,128)S(1)} copy-done((f32[4,1,256,32]{2,3,1,0:T(8,128)S(1)}, f32[4,1,256,32]{2,3,1,0:T(8,128)}, u32[]{:S(2)}) %copy-start.1) | copy-done | bytes 131096
  20.0 0.0 copy-start.2
  20.0 0.9 %copy-done.2 = f32[2,256,128]{2,1,0:T(8,128)S(1)} copy-done((f32[2,256,128]{2,1,0:T(8,128)S(1)}, f32[2,256,128]{2,1,0:T(8,128)}, u32[]{:S(2)}) %copy-start.2) | copy-done | bytes 262168
  20.9 0.0 copy-start.3
  20.9 0.9 %copy-done.3 = f32[2,256,128]{2,1,0:T(8,128)S(1)} copy-done((f32[2,256,128]{2,1,0:T(8,128)S(1)}, f32[2,256,128]{2,1,0:T(8,128)}, u32[]{:S(2)}) %copy-start.3) | copy-done | bytes 262168
  21.9 0.0 copy-start.4
  21.9 0.8 %copy-done.4 = f32[2,32,256]{2,1,0:T(8,128)S(1)} copy-done((f32[2,32,256]{2,1,0:T(8,128)S(1)}, f32[2,32,256]{2,1,0:T(8,128)}, u32[]{:S(2)}) %copy-start.4) | copy-done | bytes 65560
  22.7 41.3 %panels.1 = (f32[4,1024,128]{2,1,0:T(8,128)}, f32[4,32,256]{2,1,0:T(8,128)}) custom-call(f32[4,256,128]{2,1,0:T(8,128)S(1)} %bitcast.11, f32[2,256,128]{2,1,0:T(8,128)S(1)} %copy-done.2, f32[2,256,128]{2,1,0:T(8,128)S(1)} %copy-done.3, f32[4,32,256]{2,1,0:T(8,128)S(1)} %bitcast.13, f32[2,32,256]{2,1,0:T(8,128)S(1)} %copy-done.4), custom_call_target="tpu_custom_call" | custom-call | tf_op jit(solution)/shard_map/panels/pallas_call | solution.py:282
Async XLA Ops:
  18.0 1.0 %copy-start = (f32[4,1,256,128]{3,2,1,0:T(8,128)S(1)}, f32[4,1,256,128]{3,2,1,0:T(8,128)}, u32[]{:S(2)}) copy-start(f32[4,1,256,128]{3,2,1,0:T(8,128)} %param.2) | copy-start | bytes 1572868
  19.1 0.9 %copy-start.1 = (f32[4,1,256,32]{2,3,1,0:T(8,128)S(1)}, f32[4,1,256,32]{2,3,1,0:T(8,128)}, u32[]{:S(2)}) copy-start(f32[4,1,256,32]{2,3,1,0:T(8,128)} %param.3) | copy-start | bytes 393220
  20.0 0.9 %copy-start.2 = (f32[2,256,128]{2,1,0:T(8,128)S(1)}, f32[2,256,128]{2,1,0:T(8,128)}, u32[]{:S(2)}) copy-start(f32[2,256,128]{2,1,0:T(8,128)} %get-tuple-element.7.hpiv) | copy-start | bytes 786436
  20.9 0.9 %copy-start.3 = (f32[2,256,128]{2,1,0:T(8,128)S(1)}, f32[2,256,128]{2,1,0:T(8,128)}, u32[]{:S(2)}) copy-start(f32[2,256,128]{2,1,0:T(8,128)} %get-tuple-element.8.hcolp) | copy-start | bytes 786436
  21.9 0.8 %copy-start.4 = (f32[2,32,256]{2,1,0:T(8,128)S(1)}, f32[2,32,256]{2,1,0:T(8,128)}, u32[]{:S(2)}) copy-start(f32[2,32,256]{2,1,0:T(8,128)} %get-tuple-element.9.hrpiv) | copy-start | bytes 196612

commit v4 on v3

--- a/solution.py
+++ b/solution.py
@@ -134,23 +134,34 @@
     ).astype(F32)
     wide = jnp.concatenate([block, eye], axis=1)
     v = [wide[8 * q : 8 * q + 8] for q in range(NB // 8)]
-    for j in range(0, NB, 2):
+    for j in range(0, NB, 4):
         q0, s = divmod(j, 8)
-        first = [spread(v[q][:, j : j + 1]) for q in range(q0, NB // 8)]
-        second = [spread(v[q][:, j + 1 : j + 2]) for q in range(q0, NB // 8)]
-        r0, r1 = v[q0][s : s + 1], v[q0][s + 1 : s + 2]
-        a, b = first[0][s : s + 1], second[0][s : s + 1]
-        b1, c = first[0][s + 1 : s + 2], second[0][s + 1 : s + 2]
-        det = a * c - b * b1
-        inv_det = 1.0 / det
-        e1 = a * r1 - b1 * r0
-        s0 = (c * r0 - b * r1) * inv_det
-        s1 = e1 * inv_det
-        rs = lax.rsqrt(a)
-        base[j : j + 1, :] = r0 * rs
-        base[j + 1 : j + 2, :] = e1 * (lax.rsqrt(det) * rs)
-        for q in range(q0 if s < 6 else q0 + 1, NB // 8):
-            v[q] = v[q] - first[q - q0] * s0 - second[q - q0] * s1
+        cols = [[spread(v[q][:, j + n : j + n + 1]) for n in range(4)] for q in range(q0, NB // 8)]
+        rows = [v[q0][s + n : s + n + 1] for n in range(4)]
+        at = [[cols[0][n][s + m : s + m + 1] for n in range(4)] for m in range(4)]
+
+        def pair(r0, r1, a, b, b1, c, where):
+            det = a * c - b * b1
+            inv_det = 1.0 / det
+            e1 = a * r1 - b1 * r0
+            rs = lax.rsqrt(a)
+            base[where : where + 1, :] = r0 * rs
+            base[where + 1 : where + 2, :] = e1 * (lax.rsqrt(det) * rs)
+            return a, b, b1, c, inv_det, (c * r0 - b * r1) * inv_det, e1 * inv_det
+
+        a, b, b1, c, inv_det, s0, s1 = pair(
+            rows[0], rows[1], at[0][0], at[0][1], at[1][0], at[1][1], j
+        )
+        u0 = [(c * at[0][n] - b * at[1][n]) * inv_det for n in (2, 3)]
+        u1 = [(a * at[1][n] - b1 * at[0][n]) * inv_det for n in (2, 3)]
+        r2, r3 = (rows[m] - at[m][0] * s0 - at[m][1] * s1 for m in (2, 3))
+        p = [[at[m][n + 2] - at[m][0] * u0[n] - at[m][1] * u1[n] for n in (0, 1)] for m in (2, 3)]
+        s2, s3 = pair(r2, r3, p[0][0], p[0][1], p[1][0], p[1][1], j + 2)[5:]
+        for q in range(q0 if s == 0 else q0 + 1, NB // 8):
+            k0, k1, k2, k3 = cols[q - q0]
+            k2 = k2 - k0 * u0[0] - k1 * u1[0]
+            k3 = k3 - k0 * u0[1] - k1 * u1[1]
+            v[q] = v[q] - k0 * s0 - k1 * s1 - k2 * s2 - k3 * s3
     return base[:, NB:]
 
 
@@ -305,7 +316,7 @@
             pltpu.VMEM((width, 2 * size), BF16),
             pltpu.VMEM((width, 2 * size), BF16),
         ],
-        compiler_params=pltpu.CompilerParams(vmem_limit_bytes=48 * 1024 * 1024),
+        compiler_params=pltpu.CompilerParams(vmem_limit_bytes=62 * 1024 * 1024),
         name="panels",
     )(pts, piv, colp, right, rpiv)
     factored = factored.reshape(tile_rows, 1, size, tile_cols, 1, size)

time: 64.4 us -> 53.7 us (0.83)
  Pallas kernels: 58.7 us -> 52.8 us
  local copies, waits for them, and re-layouts: 4.68 us -> 0 us
    pallas_call x1, Pallas kernels: 41.3 us -> 35.4 us  [per_device(): pl.pallas_call(functools.partial(main_kernel, rows_n, cols_n), out_shape=...]
    unnamed x10 -> x0, local copies, waits for them, and re-layouts: 4.68 us -> none
where the time goes in v4:
time: 53.7 us; the launch traced here: 53.6 us
  Pallas kernels  52.8 us (98%)
  between operations  0.8 us (1%)
    pallas_call x1, Pallas kernels, per_device(): pl.pallas_call(functools.partial(main_kernel, rows_n, cols_n), out_shape=...  35.4 us
    pallas_call x1, Pallas kernels, per_device(): pl.pallas_call(functools.partial(fetch_kernel, rows_n, cols_n, tile_cols)...  17.4 us

profile of v4, /device:TPU:0, one launch (start us, length us, event | category | flops | bytes accessed | tf_op | source)
XLA Modules:
  0.0 53.6 jit_solution(16149760328389926029)
XLA Ops:
  0.6 17.4 %fetch.1 = (f32[2,256,128]{2,1,0:T(8,128)}, f32[2,256,128]{2,1,0:T(8,128)}, f32[2,32,256]{2,1,0:T(8,128)}) custom-call(f32[4,256,128]{2,1,0:T(8,128)} %bitcast.10, f32[4,32,256]{2,1,0:T(8,128)} %bitcast.12), custom_call_target="tpu_custom_call" | custom-call | tf_op jit(solution)/shard_map/fetch/pallas_call | solution.py:276
  18.0 35.4 %panels.1 = (f32[4,1024,128]{2,1,0:T(8,128)}, f32[4,32,256]{2,1,0:T(8,128)}) custom-call(f32[4,256,128]{2,1,0:T(8,128)} %bitcast.11, f32[2,256,128]{2,1,0:T(8,128)} %get-tuple-element.7.hpiv, f32[2,256,128]{2,1,0:T(8,128)} %get-tuple-element.8.hcolp, f32[4,32,256]{2,1,0:T(8,128)} %bitcast.13, f32[2,32,256]{2,1,0:T(8,128)} %get-tuple-element.9.hrpiv), custom_call_target="tpu_custom_call" | custom-call | tf_op jit(solution)/shard_map/panels/pallas_call | solution.py:293
